TPU v7x, 256 devices: a whole 4x4x8 slice. The times are simulated.
256 devices in a mesh: dp: 8 (over y, core), expert: 32 (over x, z).
Axes of the slice: x: 4, y: 4, z: 8, core: 2. Of those that a mesh axis runs over, the one named last changes fastest.
Arguments:
- dense_partials: float32 [8, 1024, 4096], P('dp', None, 'expert'), may hold values from -6 to 6
- dense_param: float32 [1024, 4096], P('dp', 'expert'), may hold values from -3 to 3
- dense_m: float32 [1024, 4096], P('dp', 'expert'), may hold values from -18 to 18
- dense_v: float32 [1024, 4096], P('dp', 'expert'), may hold values from 1 to 10
- sent_inputs: bfloat16 [1024, 128, 2048], P('expert', None, 'dp'), may hold values from -6 to 6
- sent_outputs: bfloat16 [1024, 128, 1408], P('expert'), may hold values from -0.23925781 to 0.23925781
- counts: int32 [32, 32], replicated, may hold values from 0 to 128, as said below
- expert_param: float32 [32, 2048, 1408], P('expert', 'dp'), may hold values from -3 to 3
- expert_m: float32 [32, 2048, 1408], P('expert', 'dp'), may hold values from -18 to 18
- expert_v: float32 [32, 2048, 1408], P('expert', 'dp'), may hold values from 1 to 10
Outputs:
- dense_param_new: float32 [1024, 4096], P('dp', 'expert')
- dense_m_new: float32 [1024, 4096], P('dp', 'expert')
- dense_v_new: float32 [1024, 4096], P('dp', 'expert')
- expert_param_new: float32 [32, 2048, 1408], P('expert', 'dp')
- expert_m_new: float32 [32, 2048, 1408], P('expert', 'dp')
- expert_v_new: float32 [32, 2048, 1408], P('expert', 'dp')
Inputs may be any that keep to these rules, and one draw needn't show every extreme that they name: counts[j, e] is the number of live leading slots of block j * 32 + e; in every draw some expert receives 128 live slots from every token group.
All inputs are finite; a program needn't handle non-finite values.
Results may differ from a plain program's by a relative error of at most 0.0003.
Values may be sent and summed in bfloat16 or wider, within the bound.
A program may use at most 128 MiB of HBM per device.

v0:
```python
import jax
import jax.numpy as jnp
from jax import lax
from jax.sharding import PartitionSpec as P


def adamw(param, moment, second, grad):
    moment_new = 0.9 * moment + 0.1 * grad
    second_new = 0.95 * second + 0.05 * grad * grad
    corrected = moment_new / (1.0 - 0.9**10)
    scaled = jnp.sqrt(second_new / (1.0 - 0.95**10)) + 1e-08
    param_new = param - 0.01 * (corrected / scaled + 0.1 * param)
    return (param_new, moment_new, second_new)


def per_device(
    dense_partials,
    dense_param,
    dense_m,
    dense_v,
    sent_inputs,
    sent_outputs,
    counts,
    expert_param,
    expert_m,
    expert_v,
):
    summed = lax.psum_scatter(dense_partials, "dp", scatter_dimension=1, tiled=True)
    dense_grad = summed[0]
    arrived_in, arrived_out = (
        lax.all_to_all(sent_inputs, "expert", split_axis=0, concat_axis=0, tiled=True),
        lax.all_to_all(sent_outputs, "expert", split_axis=0, concat_axis=0, tiled=True),
    )
    sources = arrived_in.shape[0]
    slots = arrived_in.shape[1]
    width_in = arrived_in.shape[2]
    width_out = arrived_out.shape[2]
    column = lax.dynamic_slice_in_dim(counts, lax.axis_index("expert"), 1, 1)
    live = lax.broadcasted_iota(jnp.int32, (sources, slots), 1) < column
    masked = jnp.where(live[:, :, None], arrived_out, jnp.zeros_like(arrived_out))
    expert_grad = lax.dot_general(
        arrived_in.reshape(sources * slots, width_in),
        masked.reshape(sources * slots, width_out),
        (((0,), (0,)), ((), ())),
        preferred_element_type=jnp.float32,
    )
    dp_new, dm_new, dv_new = adamw(dense_param, dense_m, dense_v, dense_grad)
    ep_new, em_new, ev_new = adamw(expert_param, expert_m, expert_v, expert_grad[None])
    return (dp_new, dm_new, dv_new, ep_new, em_new, ev_new)


def solution(mesh):
    in_specs = (
        P("dp", None, "expert"),
        P("dp", "expert"),
        P("dp", "expert"),
        P("dp", "expert"),
        P("expert", None, "dp"),
        P("expert", None, None),
        P(),
        P("expert", "dp", None),
        P("expert", "dp", None),
        P("expert", "dp", None),
    )
    out_specs = (
        P("dp", "expert"),
        P("dp", "expert"),
        P("dp", "expert"),
        P("expert", "dp", None),
        P("expert", "dp", None),
        P("expert", "dp", None),
    )
    return jax.shard_map(
        per_device, mesh=mesh, in_specs=in_specs, out_specs=out_specs, check_vma=False
    )
```

profile of v0, /device:TPU:179, one launch (start us, length us, event | category | flops | bytes accessed | tf_op | source)
XLA Modules:
  0.0 369.2 jit_solution(5030046081515007181)
XLA Ops:
  7.2 0.0 copy-start
  7.2 56.2 %all_to_all.10 = bf16[32,128,256]{2,1,0:T(8,128)(2,1)S(1)} all-to-all(bf16[32,128,256]{2,1,0:T(8,128)(2,1)} %param.14), channel_id=1, replica_groups=mesh['dp'=8,'expert'=32] {'expert'}, dimensions={0} | all-to-all | bytes 4194304 | tf_op jit(solution)/shard_map/all_to_all | solution.py:31
  63.3 0.0 copy-start.1
  63.3 8.5 %all-to-all-start = ((bf16[32,128,1408]{2,1,0:T(8,128)(2,1)}), bf16[32,128,1408]{2,1,0:T(8,128)(2,1)}, u32[]{:S(2)}, u32[]{:S(2)}) async-start(bf16[32,128,1408]{2,1,0:T(8,128)(2,1)} %param.15), calls=%async_computation.1 | async-start | bytes 23068672 | tf_op jit(solution)/shard_map/all_to_all | solution.py:32
  71.8 0.0 reduce-scatter.2.cloned.1.call-start
  71.9 0.7 reduce-scatter.2.cloned.1.call-update
  72.6 0.0 copy-done.1
  72.6 1.5 copy.24
  74.1 0.0 copy-start.2
  74.1 3.0 copy.26
  77.2 0.0 copy-done.2
  77.2 1.5 copy.28
  78.7 0.0 copy-done
  78.7 0.2 dynamic-slice_reduce_fusion
  78.9 0.7 iota_compare_fusion
  79.5 28.6 %reduce-scatter.2.cloned.1.call-done = f32[1,128,128]{2,1,0:T(8,128)} async-done(((f32[1,1024,128]{2,1,0:T(8,128)}), f32[1,128,128]{2,1,0:T(8,128)}) %reduce-scatter.2.cloned.1.call-update) | async-done | bytes 65552 | tf_op jit(solution)/shard_map/reduce_scatter | solution.py:28
  108.1 1.6 multiply_subtract_fusion.1
  109.7 235.2 %all-to-all-done = bf16[32,128,1408]{2,1,0:T(8,128)(2,1)} async-done(((bf16[32,128,1408]{2,1,0:T(8,128)(2,1)}), bf16[32,128,1408]{2,1,0:T(8,128)(2,1)}, u32[]{:S(2)}, u32[]{:S(2)}) %all-to-all-start) | async-done | bytes 11534368 | tf_op jit(solution)/shard_map/all_to_all | solution.py:32
  345.0 11.3 %multiply_subtract_fusion = (f32[1,256,1408]{1,2,0:T(8,128)}, f32[1,256,1408]{1,2,0:T(8,128)}, f32[1,256,1408]{1,2,0:T(8,128)S(1)}) fusion(f32[1,256,1408]{1,2,0:T(8,128)} %copy.28, f32[1,256,1408]{1,2,0:T(8,128)} %copy.24, f32[1,256,1408]{1,2,0:T(8,128)} %copy.26, bf16[32,128,256]{2,1,0:T(8,128)(2,1)S(1)} %all_to_all.10, ...), kind=kOutput, calls=%fused_computation.9 | convolution fusion | flops 2963963904 | bytes 22286336 | tf_op jit(solution)/shard_map/dot_general | solution.py:41
  356.2 0.0 copy-start.3
  356.2 3.0 copy.29
  359.2 0.0 copy-done.3
  359.2 1.5 copy.30
  360.8 1.5 copy.31
Async XLA Ops:
  7.2 71.5 %copy-start = (s32[32,32]{1,0:T(8,128)S(1)}, s32[32,32]{1,0:T(8,128)}, u32[]{:S(2)}) copy-start(s32[32,32]{1,0:T(8,128)} %param.16) | copy-start | bytes 12292
  63.3 9.3 %copy-start.1 = (f32[1,256,1408]{2,1,0:T(8,128)S(1)}, f32[1,256,1408]{2,1,0:T(8,128)}, u32[]{:S(2)}) copy-start(f32[1,256,1408]{2,1,0:T(8,128)} %param.18) | copy-start | bytes 4325380
  63.3 281.6 %all-to-all-start = ((bf16[32,128,1408]{2,1,0:T(8,128)(2,1)}), bf16[32,128,1408]{2,1,0:T(8,128)(2,1)}, u32[]{:S(2)}, u32[]{:S(2)}) async-start(bf16[32,128,1408]{2,1,0:T(8,128)(2,1)} %param.15), calls=%async_computation.1 | async-start | bytes 23068672 | tf_op jit(solution)/shard_map/all_to_all | solution.py:32
  71.8 36.2 %reduce-scatter.2.cloned.1.call-start = ((), (), s32[]{:S(2)}) async-start(), calls=%async_computation.3 | async-start | bytes 589824 | tf_op jit(solution)/shard_map/reduce_scatter | solution.py:28
  74.1 3.0 copy-start.2
  356.2 3.0 copy-start.3
Sparse Core Ops, SparseCore 0:
  75.2 32.8 reduce-scatter.1
where the time goes:
time: 370 us; the launch traced here: 369 us
  waiting for transfers between devices  264 us (71%)
  blocking collectives  56.2 us (15%)
  between operations  14.1 us (4%)
  local copies, waits for them, and re-layouts  12.4 us (3%)
  matrix products  11.3 us (3%)
  starting transfers between devices  8.54 us (2%)
    all_to_all x1, waiting for transfers between devices, per_device(): lax.all_to_all(sent_outputs, 'expert', split_axis=0, concat_axis=0, tiled...  235 us
    all_to_all x1, blocking collectives, per_device(): lax.all_to_all(sent_inputs, 'expert', split_axis=0, concat_axis=0, tiled=...  56.2 us
    reduce_scatter x1, waiting for transfers between devices, per_device(): lax.psum_scatter(dense_partials, 'dp', scatter_dimension=1, tiled=True)  28.6 us
    unnamed x14, local copies, waits for them, and re-layouts  12.2 us
    dot_general x1, matrix products, per_device(): lax.dot_general(arrived_in.reshape(sources * slots, width_in), masked.res...  11.3 us
    all_to_all x1, starting transfers between devices, per_device(): lax.all_to_all(sent_outputs, 'expert', split_axis=0, concat_axis=0, tiled...  8.5 us
  transfers between devices with their start and end apart: 2, of which 2 were waited for; matrix products, arithmetic and copies ran while one was open for 2% of the time, Pallas kernels for 0%

commit v1 on v0

--- a/solution.py
+++ b/solution.py
@@ -27,20 +27,20 @@
 ):
     summed = lax.psum_scatter(dense_partials, "dp", scatter_dimension=1, tiled=True)
     dense_grad = summed[0]
-    arrived_in, arrived_out = (
-        lax.all_to_all(sent_inputs, "expert", split_axis=0, concat_axis=0, tiled=True),
-        lax.all_to_all(sent_outputs, "expert", split_axis=0, concat_axis=0, tiled=True),
-    )
-    sources = arrived_in.shape[0]
-    slots = arrived_in.shape[1]
-    width_in = arrived_in.shape[2]
-    width_out = arrived_out.shape[2]
+    replicas = lax.axis_size("dp")
+    blocks, slots, width_out = sent_outputs.shape
+    width_in = sent_inputs.shape[2]
+    part = slots // replicas
+    share = lax.dynamic_slice_in_dim(sent_outputs, lax.axis_index("dp") * part, part, 1)
+    arrived_share = lax.all_to_all(share, "expert", split_axis=0, concat_axis=0, tiled=True)
+    arrived_in = lax.all_to_all(sent_inputs, "expert", split_axis=0, concat_axis=0, tiled=True)
+    arrived_out = lax.all_gather(arrived_share, "dp")
     column = lax.dynamic_slice_in_dim(counts, lax.axis_index("expert"), 1, 1)
-    live = lax.broadcasted_iota(jnp.int32, (sources, slots), 1) < column
-    masked = jnp.where(live[:, :, None], arrived_out, jnp.zeros_like(arrived_out))
+    live = lax.broadcasted_iota(jnp.int32, (blocks, slots), 1) < column
+    masked = jnp.where(live[:, :, None], arrived_in, jnp.zeros_like(arrived_in))
     expert_grad = lax.dot_general(
-        arrived_in.reshape(sources * slots, width_in),
-        masked.reshape(sources * slots, width_out),
+        masked.reshape(blocks, replicas, part, width_in).transpose(1, 0, 2, 3).reshape(blocks * slots, width_in),
+        arrived_out.reshape(blocks * slots, width_out),
         (((0,), (0,)), ((), ())),
         preferred_element_type=jnp.float32,
     )

time: 370 us -> 148 us (0.40)
  the two profiles are of different devices: /device:TPU:179 before, /device:TPU:1 now
where the time goes in v1:
time: 148 us; the launch traced here: 147 us
  waiting for transfers between devices  93.8 us (63%)
  starting transfers between devices  19.7 us (13%)
  between operations  14.1 us (10%)
  matrix products  12.5 us (8%)
  local copies, waits for them, and re-layouts  3.89 us (3%)
  other arithmetic  3.39 us (2%)
    all_to_all x1, waiting for transfers between devices, per_device(): lax.all_to_all(sent_inputs, 'expert', split_axis=0, concat_axis=0, tiled=...  46.8 us
    all_to_all x1, waiting for transfers between devices, per_device(): lax.all_to_all(share, 'expert', split_axis=0, concat_axis=0, tiled=True)  33.2 us
    all_gather x1, waiting for transfers between devices, per_device(): arrived_out = lax.all_gather(arrived_share, 'dp')  13 us
    dot_general x1, matrix products, per_device(): lax.dot_general(masked.reshape(blocks, replicas, part, width_in).transpos...  12.5 us
    all_to_all x1, starting transfers between devices, per_device(): lax.all_to_all(share, 'expert', split_axis=0, concat_axis=0, tiled=True)  11.9 us
    all_to_all x1, starting transfers between devices, per_device(): lax.all_to_all(sent_inputs, 'expert', split_axis=0, concat_axis=0, tiled=...  7.76 us
  transfers between devices with their start and end apart: 4, of which 3 were waited for; matrix products, arithmetic and copies ran while one was open for 2% of the time, Pallas kernels for 0%

profile of v1, /device:TPU:1, one launch (start us, length us, event | category | flops | bytes accessed | tf_op | source)
XLA Modules:
  0.0 147.4 jit_solution(2052729192891371510)
XLA Ops:
  7.2 0.0 copy-start
  7.2 2.6 %constant_dynamic-slice_fusion = bf16[32,16,1408]{2,1,0:T(8,128)(2,1)} fusion(bf16[32,128,1408]{2,1,0:T(8,128)(2,1)} %param.15, s32[]{:T(128)S(6)} %select_n.12), kind=kLoop, calls=%fused_computation.16 | loop fusion | bytes 2883588 | tf_op jit(solution)/shard_map/dynamic_slice | solution.py:34
  9.8 11.9 %all-to-all-start.1 = ((bf16[32,16,1408]{2,1,0:T(8,128)(2,1)}), bf16[32,16,1408]{2,1,0:T(8,128)(2,1)S(1)}, u32[]{:S(2)}, u32[]{:S(2)}) async-start(bf16[32,16,1408]{2,1,0:T(8,128)(2,1)} %constant_dynamic-slice_fusion), calls=%async_computation.2 | async-start | bytes 2883584 | tf_op jit(solution)/shard_map/all_to_all | solution.py:35
  21.6 0.0 reduce-scatter.2.cloned.1.call-start
  21.7 0.7 reduce-scatter.2.cloned.1.call-update
  22.4 0.0 all-gather.3.cloned.1.call-start
  22.4 33.2 %all-to-all-done.1 = bf16[32,16,1408]{2,1,0:T(8,128)(2,1)S(1)} async-done(((bf16[32,16,1408]{2,1,0:T(8,128)(2,1)}), bf16[32,16,1408]{2,1,0:T(8,128)(2,1)S(1)}, u32[]{:S(2)}, u32[]{:S(2)}) %all-to-all-start.1) | async-done | bytes 1441824 | tf_op jit(solution)/shard_map/all_to_all | solution.py:35
  55.7 0.0 copy-start.1
  55.7 1.1 copy-done.1
  56.8 0.0 all-gather.3.cloned.1.call-update
  56.8 0.0 copy-start.2
  56.8 0.0 copy-start.3
  56.8 0.0 copy-start.4
  56.8 7.8 %all-to-all-start = ((bf16[32,128,256]{2,1,0:T(8,128)(2,1)}), bf16[32,128,256]{2,1,0:T(8,128)(2,1)S(1)}, u32[]{:S(2)}, u32[]{:S(2)}) async-start(bf16[32,128,256]{2,1,0:T(8,128)(2,1)} %param.14), calls=%async_computation.1 | async-start | bytes 4194304 | tf_op jit(solution)/shard_map/all_to_all | solution.py:36
  64.6 0.0 copy-done
  64.6 0.2 dynamic-slice_reduce_fusion
  64.8 0.1 iota_compare_fusion
  64.9 0.0 reduce-scatter.2.cloned.1.call-done
  64.9 0.0 copy-done.2
  64.9 0.0 copy-done.3
  64.9 0.0 copy-done.4
  64.9 1.5 %multiply_subtract_fusion.1 = (f32[128,128]{1,0:T(8,128)}, f32[128,128]{1,0:T(8,128)}, f32[128,128]{1,0:T(8,128)}) fusion(f32[128,128]{1,0:T(8,128)S(1)} %copy-done.2, f32[1,128,128]{2,1,0:T(8,128)} %reduce-scatter.2.cloned.1.call-done, f32[128,128]{1,0:T(8,128)S(1)} %copy-done.3, f32[128,128]{1,0:T(8,128)S(1)} %copy-done.4), kind=kLoop, calls=%fused_computation.13 | loop fusion | flops 245760 | bytes 458752 | tf_op jit(solution)/shard_map/sub | solution.py:12
  66.4 46.8 %all-to-all-done = bf16[32,128,256]{2,1,0:T(8,128)(2,1)S(1)} async-done(((bf16[32,128,256]{2,1,0:T(8,128)(2,1)}), bf16[32,128,256]{2,1,0:T(8,128)(2,1)S(1)}, u32[]{:S(2)}, u32[]{:S(2)}) %all-to-all-start) | async-done | bytes 2097184 | tf_op jit(solution)/shard_map/all_to_all | solution.py:36
  113.3 1.8 %broadcast_select_fusion = bf16[32,128,256]{2,1,0:T(8,128)(2,1)} fusion(bf16[32,128,256]{2,1,0:T(8,128)(2,1)S(1)} %all-to-all-done, pred[32,128]{1,0:T(8,128)(4,1)S(1)} %iota_compare_fusion), kind=kLoop, calls=%fused_computation.4 | loop fusion | flops 1048576 | bytes 4198400 | tf_op jit(solution)/shard_map/jit(_where)/select_n | solution.py:40
  115.1 13.0 %all-gather.3.cloned.1.call-done = bf16[256,16,1408]{2,1,0:T(8,128)(2,1)} async-done(((bf16[32,16,1408]{2,1,0:T(8,128)(2,1)}), bf16[256,16,1408]{2,1,0:T(8,128)(2,1)}) %all-gather.3.cloned.1.call-update) | async-done | bytes 11534352 | tf_op jit(solution)/shard_map/all_gather | solution.py:37
  128.1 12.5 %multiply_subtract_fusion = (f32[1,256,1408]{2,1,0:T(8,128)}, f32[1,256,1408]{2,1,0:T(8,128)}, f32[1,256,1408]{2,1,0:T(8,128)}) fusion(f32[1,256,1408]{2,1,0:T(8,128)} %param.17, f32[1,256,1408]{2,1,0:T(8,128)} %param.18, f32[1,256,1408]{2,1,0:T(8,128)} %param.19, bf16[8,32,16,1408]{3,2,1,0:T(8,128)(2,1)} %bitcast.28, bf16[32,8,16,256]{3,2,1,0:T(8,128)(2,1)} %bitcast.27), kind=kOutput, calls=%fused_computation.8 | convolution fusion | flops 2958196736 | bytes 22282240 | tf_op jit(solution)/shard_map/dot_general | solution.py:41
Async XLA Ops:
  7.2 57.4 %copy-start = (s32[32,32]{1,0:T(8,128)S(1)}, s32[32,32]{1,0:T(8,128)}, u32[]{:S(2)}) copy-start(s32[32,32]{1,0:T(8,128)} %param.16) | copy-start | bytes 12292
  9.8 45.9 %all-to-all-start.1 = ((bf16[32,16,1408]{2,1,0:T(8,128)(2,1)}), bf16[32,16,1408]{2,1,0:T(8,128)(2,1)S(1)}, u32[]{:S(2)}, u32[]{:S(2)}) async-start(bf16[32,16,1408]{2,1,0:T(8,128)(2,1)} %constant_dynamic-slice_fusion), calls=%async_computation.2 | async-start | bytes 2883584 | tf_op jit(solution)/shard_map/all_to_all | solution.py:35
  21.6 43.2 %reduce-scatter.2.cloned.1.call-start = ((), (), s32[]{:S(2)}) async-start(), calls=%async_computation.3 | async-start | bytes 589824 | tf_op jit(solution)/shard_map/reduce_scatter | solution.py:28
  22.4 105.7 %all-gather.3.cloned.1.call-start = ((), (), s32[]{:S(2)}) async-start(), calls=%async_computation.4 | async-start | bytes 12976128 | tf_op jit(solution)/shard_map/all_gather | solution.py:37
  55.7 1.1 copy-start.1
  56.8 8.1 %copy-start.2 = (f32[128,128]{1,0:T(8,128)S(1)}, f32[128,128]{1,0:T(8,128)}, u32[]{:S(2)}) copy-start(f32[128,128]{1,0:T(8,128)} %param.11) | copy-start | bytes 196612
  56.8 8.1 %copy-start.3 = (f32[128,128]{1,0:T(8,128)S(1)}, f32[128,128]{1,0:T(8,128)}, u32[]{:S(2)}) copy-start(f32[128,128]{1,0:T(8,128)} %param.12) | copy-start | bytes 196612
  56.8 8.1 %copy-start.4 = (f32[128,128]{1,0:T(8,128)S(1)}, f32[128,128]{1,0:T(8,128)}, u32[]{:S(2)}) copy-start(f32[128,128]{1,0:T(8,128)} %param.13) | copy-start | bytes 196612
  56.8 56.5 %all-to-all-start = ((bf16[32,128,256]{2,1,0:T(8,128)(2,1)}), bf16[32,128,256]{2,1,0:T(8,128)(2,1)S(1)}, u32[]{:S(2)}, u32[]{:S(2)}) async-start(bf16[32,128,256]{2,1,0:T(8,128)(2,1)} %param.14), calls=%async_computation.1 | async-start | bytes 4194304 | tf_op jit(solution)/shard_map/all_to_all | solution.py:36
Sparse Core Ops, SparseCore 0:
  25.0 33.4 reduce-scatter.1
  61.0 66.9 all-gather.2

commit v2 on v1

v2 whole, which is shorter than its diff:
```python
import jax
import jax.numpy as jnp
from jax import lax
from jax.experimental import pallas as pl
from jax.experimental.pallas import tpu as pltpu
from jax.sharding import PartitionSpec as P

MESH = pl.DeviceIdType.MESH
X, Z, Y = 4, 8, 4
DP = 2 * Y
BF16_ROWS = 16


def adamw(param, moment, second, grad):
    moment_new = 0.9 * moment + 0.1 * grad
    second_new = 0.95 * second + 0.05 * grad * grad
    corrected = moment_new / (1.0 - 0.9**10)
    scaled = jnp.sqrt(second_new / (1.0 - 0.95**10)) + 1e-08
    param_new = param - 0.01 * (corrected / scaled + 0.1 * param)
    return (param_new, moment_new, second_new)


def wave(k):
    half = (k + 1) // 2
    return 4 + half if k % 2 == 0 else 4 - half


def exchange(
    counts,
    partials,
    inputs,
    outputs,
    grad,
    dense,
    ins,
    outs,
    rows,
    out_send,
    out_recv,
    in_send,
    in_recv,
    row_send,
    row_recv,
    y_send,
    y_recv,
    core_send,
    core_recv,
):
    d, e = lax.axis_index("dp"), lax.axis_index("expert")
    y, c = d // 2, d % 2
    x, z = e // Z, e % Z
    ahead = lax.rem(y + 1 + 2 * c, Y)
    behind = lax.rem(y + 3 - 2 * c, Y)
    across = lax.rem(y + 2, Y)
    sibling = 2 * y + 1 - c

    def remote(src, dst, send, recv, dp, expert):
        return pltpu.make_async_remote_copy(
            src_ref=src,
            dst_ref=dst,
            send_sem=send,
            recv_sem=recv,
            device_id=(dp, expert),
            device_id_type=MESH,
        )

    def peer(dx, dz):
        return lax.rem(x + dx, X) * Z + lax.rem(z + dz, Z)

    barrier = pltpu.get_barrier_semaphore()
    for dx in range(X):
        for dz in range(Z):
            if dx or dz:
                pl.semaphore_signal(barrier, inc=1, device_id=(d, peer(dx, dz)), device_id_type=MESH)
    for step in range(1, DP):
        pl.semaphore_signal(barrier, inc=1, device_id=(lax.rem(d + step, DP), e), device_id_type=MESH)
    pl.semaphore_wait(barrier, X * Z - 1 + DP - 1)

    def send_wave(k, src_of, buffer, send, recv):
        dz = wave(k)
        slot = z * X + x
        for dx in (2, 1, 3, 0):
            there = peer(dx, dz)
            if dx or dz:
                remote(src_of(there), buffer(slot), send, recv.at[z], d, there).start()
            else:
                pltpu.make_async_copy(src_of(there), buffer(slot), recv.at[z]).start()

    def arrived(k):
        from_z = lax.rem(z + Z - wave(k), Z)
        return from_z, pl.ds(pl.multiple_of(from_z * X, X), X)

    def wait_recv(ref, recv):
        remote(ref, ref, recv, recv, d, e).wait_recv()

    def out_src(there):
        return outputs.at[there, d]

    def in_src(there):
        return inputs.at[there]

    for k in range(Z):
        send_wave(k, out_src, lambda slot: outs.at[d, slot], out_send, out_recv)
    for step in range(1, DP):
        there = lax.rem(d + step, DP)
        remote(partials.at[there], rows.at[d], row_send, row_recv, there, e).start()
    pltpu.make_async_copy(partials.at[d], rows.at[d], row_recv).start()

    def own(k):
        from_z, slots = arrived(k)
        piece = outs.at[d, slots]
        wait_recv(piece, out_recv.at[from_z])
        remote(piece, piece, y_send, y_recv.at[k, 0], 2 * ahead + c, e).start()
        remote(piece, piece, y_send, y_recv.at[k, 1], 2 * behind + c, e).start()
        remote(piece, piece, core_send, core_recv.at[k, 0], sibling, e).start()

    def near(k):
        _, slots = arrived(k)
        piece = outs.at[2 * behind + c, slots]
        wait_recv(piece, y_recv.at[k, 0])
        remote(piece, piece, y_send, y_recv.at[k, 2], 2 * ahead + c, e).start()
        remote(piece, piece, core_send, core_recv.at[k, 1], sibling, e).start()
        piece = outs.at[2 * ahead + c, slots]
        wait_recv(piece, y_recv.at[k, 1])
        remote(piece, piece, core_send, core_recv.at[k, 2], sibling, e).start()

    def far(k):
        _, slots = arrived(k)
        piece = outs.at[2 * across + c, slots]
        wait_recv(piece, y_recv.at[k, 2])
        remote(piece, piece, core_send, core_recv.at[k, 3], sibling, e).start()

    for k in range(Z + 2):
        if k < Z:
            own(k)
            send_wave(k, in_src, lambda slot: ins.at[:, slot], in_send, in_recv)
        if 1 <= k <= Z:
            near(k - 1)
        if k >= 2:
            far(k - 2)

    wait_recv(rows, row_recv)
    total = rows[0]
    for step in range(1, DP):
        total = total + rows[step]
    dense[...] = total

    for k in range(Z):
        from_z, slots = arrived(k)
        wait_recv(outs.at[sibling, slots], core_recv.at[k, 0])
        wait_recv(outs.at[2 * ahead + 1 - c, slots], core_recv.at[k, 1])
        wait_recv(outs.at[2 * behind + 1 - c, slots], core_recv.at[k, 2])
        wait_recv(outs.at[2 * across + 1 - c, slots], core_recv.at[k, 3])
        wait_recv(ins.at[:, slots], in_recv.at[from_z])
        live = []
        for from_x in range(X):
            block = ins[:, from_z * X + from_x]
            slot = BF16_ROWS * lax.broadcasted_iota(jnp.int32, block.shape, 0) + lax.broadcasted_iota(jnp.int32, block.shape, 1)
            live.append(jnp.where(slot < counts[from_x * Z + from_z, e], block, jnp.zeros_like(block)))
        left = jnp.stack(live, axis=1)
        right = outs[:, slots]
        product = lax.dot_general(
            left.reshape(-1, left.shape[-1]),
            right.reshape(-1, right.shape[-1]),
            (((0,), (0,)), ((), ())),
            preferred_element_type=jnp.float32,
        )
        if k == 0:
            grad[...] = product
        else:
            grad[...] += product

    def wait_send(ref, send):
        remote(ref, ref, send, send, d, e).wait_send()

    wait_send(outs.at[0, pl.ds(0, X * Z - 1)], out_send)
    wait_send(ins.at[:, pl.ds(0, X * Z - 1)], in_send)
    wait_send(rows.at[pl.ds(0, DP - 1)], row_send)
    wait_send(outs.at[pl.ds(0, 3)], y_send)
    wait_send(outs.at[pl.ds(0, 4)], core_send)


def per_device(
    dense_partials,
    dense_param,
    dense_m,
    dense_v,
    sent_inputs,
    sent_outputs,
    counts,
    expert_param,
    expert_m,
    expert_v,
):
    blocks, slots, width_in = sent_inputs.shape
    width_out = sent_outputs.shape[2]
    part = slots // DP
    dense_rows, dense_width = dense_partials.shape[1] // DP, dense_partials.shape[2]
    dma = pltpu.SemaphoreType.DMA
    expert_grad, dense_grad = pl.pallas_call(
        exchange,
        name="exchange",
        out_shape=(
            jax.ShapeDtypeStruct((width_in, width_out), jnp.float32),
            jax.ShapeDtypeStruct((dense_rows, dense_width), jnp.float32),
        ),
        in_specs=[pl.BlockSpec(memory_space=pltpu.SMEM)] + [pl.BlockSpec(memory_space=pl.ANY)] * 3,
        out_specs=(pl.BlockSpec(memory_space=pltpu.VMEM),) * 2,
        scratch_shapes=[
            pltpu.VMEM((DP, blocks, part, width_in), jnp.bfloat16),
            pltpu.VMEM((DP, blocks, part, width_out), jnp.bfloat16),
            pltpu.VMEM((DP, dense_rows, dense_width), jnp.float32),
            dma,
            dma((Z,)),
            dma,
            dma((Z,)),
            dma,
            dma,
            dma,
            dma((Z, 3)),
            dma,
            dma((Z, 4)),
        ],
        cost_estimate=pl.CostEstimate(
            flops=2 * blocks * slots * width_in * width_out,
            bytes_accessed=2 * blocks * slots * (width_in + width_out),
            transcendentals=0,
        ),
        compiler_params=pltpu.CompilerParams(collective_id=0, has_side_effects=True, vmem_limit_bytes=48 << 20),
    )(
        counts,
        dense_partials.reshape(DP, dense_rows, dense_width),
        sent_inputs.reshape(blocks, DP, part, width_in),
        sent_outputs.reshape(blocks, DP, part, width_out),
    )
    dp_new, dm_new, dv_new = adamw(dense_param, dense_m, dense_v, dense_grad)
    ep_new, em_new, ev_new = adamw(expert_param, expert_m, expert_v, expert_grad[None])
    return (dp_new, dm_new, dv_new, ep_new, em_new, ev_new)


def solution(mesh):
    in_specs = (
        P("dp", None, "expert"),
        P("dp", "expert"),
        P("dp", "expert"),
        P("dp", "expert"),
        P("expert", None, "dp"),
        P("expert", None, None),
        P(),
        P("expert", "dp", None),
        P("expert", "dp", None),
        P("expert", "dp", None),
    )
    out_specs = (
        P("dp", "expert"),
        P("dp", "expert"),
        P("dp", "expert"),
        P("expert", "dp", None),
        P("expert", "dp", None),
        P("expert", "dp", None),
    )
    return jax.shard_map(per_device, mesh=mesh, in_specs=in_specs, out_specs=out_specs, check_vma=False)
```

time: 148 us -> 100 us (0.68)
  waiting for transfers between devices: 93.8 us -> 0 us
  Pallas kernels: 0 us -> 92.3 us
  starting transfers between devices: 19.7 us -> 0 us
  between operations: 14.1 us -> 0.71 us
  matrix products: 12.5 us -> 0 us
    pallas_call x0 -> x1, Pallas kernels: none -> 92.3 us  [per_device(): pl.pallas_call(exchange, name='exchange', out_shape=(jax.ShapeDtypeStruct...]
    all_to_all x2 -> x0, waiting for transfers between devices: 80.1 us -> none  [the longest x1 46.8 us: per_device(): lax.all_to_all(sent_inputs, 'expert', split_axis=0, concat_axis=0, tiled=...]
    all_to_all x2 -> x0, starting transfers between devices: 19.6 us -> none  [the longest x1 11.9 us: per_device(): lax.all_to_all(share, 'expert', split_axis=0, concat_axis=0, tiled=True)]
    all_gather x1 -> x0, waiting for transfers between devices: 13 us -> none  [per_device(): arrived_out = lax.all_gather(arrived_share, 'dp')]
    dot_general x1 -> x0, matrix products: 12.5 us -> none  [per_device(): lax.dot_general(masked.reshape(blocks, replicas, part, width_in).transpos...]
    dynamic_slice x2 -> x0, local copies, waits for them, and re-layouts: 2.76 us -> none  [the longest x1 2.58 us: per_device(): lax.dynamic_slice_in_dim(sent_outputs, lax.axis_index('dp') * part, part, 1)]
    unnamed x10 -> x18, local copies, waits for them, and re-layouts: 1.13 us -> 3.37 us
    sub x1 -> x2, other arithmetic: 1.54 us -> 3.43 us  [adamw(): param_new = param - 0.01 * (corrected / scaled + 0.1 * param)]
  transfers between devices with their start and end apart: 4 -> 0, of which waited for: 3 -> 0; matrix products, arithmetic and copies ran while one was open for 2% -> 0% of each run, Pallas kernels for 0% -> 0%
where the time goes in v2:
time: 100 us; the launch traced here: 99.8 us
  Pallas kernels  92.3 us (92%)
  other arithmetic  3.43 us (3%)
  local copies, waits for them, and re-layouts  3.37 us (3%)
    pallas_call x1, Pallas kernels, per_device(): pl.pallas_call(exchange, name='exchange', out_shape=(jax.ShapeDtypeStruct...  92.3 us
    sub x2, other arithmetic, adamw(): param_new = param - 0.01 * (corrected / scaled + 0.1 * param)  3.43 us
    unnamed x18, local copies, waits for them, and re-layouts  3.37 us

profile of v2, /device:TPU:1, one launch (start us, length us, event | category | flops | bytes accessed | tf_op | source)
XLA Modules:
  0.0 99.8 jit_solution(8931621053131192531)
XLA Ops:
  0.6 0.0 copy-start
  0.6 1.6 %copy-done = bf16[32,128,256]{2,1,0:T(8,128)(2,1)S(1)} copy-done((bf16[32,128,256]{2,1,0:T(8,128)(2,1)S(1)}, bf16[32,128,256]{2,1,0:T(8,128)(2,1)}, u32[]{:S(2)}) %copy-start) | copy-done | bytes 2097176
  2.2 0.0 copy-start.1
  2.2 1.0 %copy-done.1 = f32[1,1024,128]{2,1,0:T(8,128)S(1)} copy-done((f32[1,1024,128]{2,1,0:T(8,128)S(1)}, f32[1,1024,128]{2,1,0:T(8,128)}, u32[]{:S(2)}) %copy-start.1) | copy-done | bytes 524312
  3.3 0.0 copy-start.2
  3.3 0.7 copy-done.2
  4.0 0.0 copy-start.3
  4.0 0.0 copy-start.4
  4.0 0.0 copy-start.5
  4.0 92.3 %exchange.1 = (f32[256,1408]{1,0:T(8,128)S(1)}, f32[128,128]{1,0:T(8,128)S(1)}) custom-call(s32[32,32]{1,0:T(8,128)S(1)} %copy-done.2, f32[8,128,128]{2,1,0:T(8,128)S(1)} %bitcast.12, bf16[32,8,16,256]{3,2,1,0:T(8,128)(2,1)S(1)} %bitcast.11, bf16[32,8,16,1408]{3,2,1,0:T(8,128)(2,1)} %bitcast.13), custom_call_target="tpu_custom_call" | custom-call | flops 2952790016 | bytes 13631488 | tf_op jit(solution)/shard_map/exchange/pallas_call | solution.py:200
  96.3 0.0 copy-done.3
  96.3 0.0 copy-done.4
  96.3 0.0 copy-done.5
  96.3 0.0 copy-start.6
  96.3 0.0 copy-start.7
  96.3 0.0 copy-start.8
  96.3 2.7 %multiply_subtract_fusion = (f32[1,256,1408]{2,1,0:T(8,128)}, f32[1,256,1408]{2,1,0:T(8,128)}, f32[1,256,1408]{2,1,0:T(8,128)}) fusion(f32[1,256,1408]{2,1,0:T(8,128)S(1)} %copy-done.3, f32[256,1408]{1,0:T(8,128)S(1)} %get-tuple-element.9, f32[1,256,1408]{2,1,0:T(8,128)S(1)} %copy-done.4, f32[1,256,1408]{2,1,0:T(8,128)S(1)} %copy-done.5), kind=kLoop, calls=%fused_computation.4 | loop fusion | flops 5406720 | bytes 10092544 | tf_op jit(solution)/shard_map/sub | solution.py:19
  99.1 0.0 copy-done.6
  99.1 0.0 copy-done.7
  99.1 0.0 copy-done.8
  99.1 0.7 multiply_subtract_fusion.1
Async XLA Ops:
  0.6 1.6 %copy-start = (bf16[32,128,256]{2,1,0:T(8,128)(2,1)S(1)}, bf16[32,128,256]{2,1,0:T(8,128)(2,1)}, u32[]{:S(2)}) copy-start(bf16[32,128,256]{2,1,0:T(8,128)(2,1)} %param.14) | copy-start | bytes 6291460
  2.2 1.0 %copy-start.1 = (f32[1,1024,128]{2,1,0:T(8,128)S(1)}, f32[1,1024,128]{2,1,0:T(8,128)}, u32[]{:S(2)}) copy-start(f32[1,1024,128]{2,1,0:T(8,128)} %param.10) | copy-start | bytes 1572868
  3.3 0.7 copy-start.2
  4.0 92.3 %copy-start.3 = (f32[1,256,1408]{2,1,0:T(8,128)S(1)}, f32[1,256,1408]{2,1,0:T(8,128)}, u32[]{:S(2)}) copy-start(f32[1,256,1408]{2,1,0:T(8,128)} %param.17) | copy-start | bytes 4325380
  4.0 92.3 %copy-start.4 = (f32[1,256,1408]{2,1,0:T(8,128)S(1)}, f32[1,256,1408]{2,1,0:T(8,128)}, u32[]{:S(2)}) copy-start(f32[1,256,1408]{2,1,0:T(8,128)} %param.18) | copy-start | bytes 4325380
  4.0 92.3 %copy-start.5 = (f32[1,256,1408]{2,1,0:T(8,128)S(1)}, f32[1,256,1408]{2,1,0:T(8,128)}, u32[]{:S(2)}) copy-start(f32[1,256,1408]{2,1,0:T(8,128)} %param.19) | copy-start | bytes 4325380
  96.3 2.8 %copy-start.6 = (f32[128,128]{1,0:T(8,128)S(1)}, f32[128,128]{1,0:T(8,128)}, u32[]{:S(2)}) copy-start(f32[128,128]{1,0:T(8,128)} %param.11) | copy-start | bytes 196612
  96.3 2.8 %copy-start.7 = (f32[128,128]{1,0:T(8,128)S(1)}, f32[128,128]{1,0:T(8,128)}, u32[]{:S(2)}) copy-start(f32[128,128]{1,0:T(8,128)} %param.12) | copy-start | bytes 196612
  96.3 2.8 %copy-start.8 = (f32[128,128]{1,0:T(8,128)S(1)}, f32[128,128]{1,0:T(8,128)}, u32[]{:S(2)}) copy-start(f32[128,128]{1,0:T(8,128)} %param.13) | copy-start | bytes 196612

commit v3 on v2

v3 whole, which is shorter than its diff:
```python
import jax
import jax.numpy as jnp
from jax import lax
from jax.experimental import pallas as pl
from jax.experimental.pallas import tpu as pltpu
from jax.sharding import PartitionSpec as P

MESH = pl.DeviceIdType.MESH
X, Z, Y = 4, 8, 4
DP = 2 * Y
BF16_ROWS = 16


def adamw(param, moment, second, grad):
    moment_new = 0.9 * moment + 0.1 * grad
    second_new = 0.95 * second + 0.05 * grad * grad
    corrected = moment_new / (1.0 - 0.9**10)
    scaled = jnp.sqrt(second_new / (1.0 - 0.95**10)) + 1e-08
    param_new = param - 0.01 * (corrected / scaled + 0.1 * param)
    return (param_new, moment_new, second_new)


def wave(k):
    half = (k + 1) // 2
    return 4 + half if k % 2 == 0 else 4 - half


def exchange(
    counts_hbm,
    partials,
    inputs,
    outputs,
    grad,
    dense,
    counts,
    ins,
    outs,
    relay_ins,
    relay_outs,
    rows,
    counts_sem,
    send,
    x_out_recv,
    x_in_recv,
    out_recv,
    in_recv,
    row_recv,
    y_recv,
    core_recv,
):
    d, e = lax.axis_index("dp"), lax.axis_index("expert")
    y, c = d // 2, d % 2
    x, z = e // Z, e % Z
    ahead = lax.rem(y + 1 + 2 * c, Y)
    behind = lax.rem(y + 3 - 2 * c, Y)
    across = lax.rem(y + 2, Y)
    sibling = 2 * y + 1 - c
    to_x, to_z, to_y, to_core, to_rows = (send.at[i] for i in range(5))

    def remote(src, dst, send, recv, dp, expert):
        return pltpu.make_async_remote_copy(
            src_ref=src,
            dst_ref=dst,
            send_sem=send,
            recv_sem=recv,
            device_id=(dp, expert),
            device_id_type=MESH,
        )

    def peer(dx, dz):
        return lax.rem(x + dx, X) * Z + lax.rem(z + dz, Z)

    load_counts = pltpu.make_async_copy(counts_hbm, counts, counts_sem)
    load_counts.start()
    barrier = pltpu.get_barrier_semaphore()
    for dz in range(1, Z):
        pl.semaphore_signal(barrier, inc=1, device_id=(d, peer(0, dz)), device_id_type=MESH)
    for dx in range(1, X):
        pl.semaphore_signal(barrier, inc=1, device_id=(d, peer(dx, 0)), device_id_type=MESH)
    for step in range(1, DP):
        pl.semaphore_signal(barrier, inc=1, device_id=(lax.rem(d + step, DP), e), device_id_type=MESH)
    pl.semaphore_wait(barrier, Z - 1 + X - 1 + DP - 1)

    def slot_of(source_z, dx):
        return source_z * X + dx

    def slots_from(k):
        return pl.ds(pl.multiple_of(lax.rem(z + Z - wave(k), Z) * X, X), X)

    def wait_recv(ref, recv):
        remote(ref, ref, recv, recv, d, e).wait_recv()

    def to_columns(k, src_of, buffer, relay, x_recv, recv):
        for dx in (2, 1, 3):
            block = src_of(peer(dx, wave(k)))
            if wave(k):
                remote(block, relay.at[k, dx - 1], to_x, x_recv.at[k], d, peer(dx, 0)).start()
            else:
                remote(block, buffer(pl.ds(slot_of(z, dx), 1)).at[0], to_x, recv.at[k], d, peer(dx, 0)).start()

    def own_column(k, src_of, buffer, recv):
        there = peer(0, wave(k))
        mine = buffer(pl.ds(slot_of(z, 0), 1)).at[0]
        if wave(k):
            remote(src_of(there), mine, to_z, recv.at[k], d, there).start()
        else:
            pltpu.make_async_copy(src_of(there), mine, recv.at[k]).start()

    def relay_column(k, buffer, relay, x_recv, recv):
        if wave(k):
            wait_recv(relay.at[k], x_recv.at[k])
            remote(relay.at[k], buffer(pl.ds(slot_of(z, 1), X - 1)), to_z, recv.at[k], d, peer(0, wave(k))).start()

    def out_src(there):
        return outputs.at[there, d]

    def out_at(slots):
        return outs.at[d, slots]

    def in_src(there):
        return inputs.at[there]

    def in_at(slots):
        return ins.at[slots]

    for k in range(Z):
        own_column(k, out_src, out_at, out_recv)
        to_columns(k, out_src, out_at, relay_outs, x_out_recv, out_recv)
    for step in range(1, DP):
        there = lax.rem(d + step, DP)
        remote(partials.at[there], rows.at[d], to_rows, row_recv, there, e).start()
    pltpu.make_async_copy(partials.at[d], rows.at[d], row_recv).start()

    def own(k):
        piece = outs.at[d, slots_from(k)]
        wait_recv(piece, out_recv.at[k])
        remote(piece, piece, to_y, y_recv.at[k, 0], 2 * ahead + c, e).start()
        remote(piece, piece, to_y, y_recv.at[k, 1], 2 * behind + c, e).start()
        remote(piece, piece, to_core, core_recv.at[k, 0], sibling, e).start()

    def near(k):
        piece = outs.at[2 * behind + c, slots_from(k)]
        wait_recv(piece, y_recv.at[k, 0])
        remote(piece, piece, to_y, y_recv.at[k, 2], 2 * ahead + c, e).start()
        remote(piece, piece, to_core, core_recv.at[k, 1], sibling, e).start()
        piece = outs.at[2 * ahead + c, slots_from(k)]
        wait_recv(piece, y_recv.at[k, 1])
        remote(piece, piece, to_core, core_recv.at[k, 2], sibling, e).start()

    def far(k):
        piece = outs.at[2 * across + c, slots_from(k)]
        wait_recv(piece, y_recv.at[k, 2])
        remote(piece, piece, to_core, core_recv.at[k, 3], sibling, e).start()

    for i in range(Z + 5):
        if i < Z:
            relay_column(i, out_at, relay_outs, x_out_recv, out_recv)
            to_columns(i, in_src, in_at, relay_ins, x_in_recv, in_recv)
        if 3 <= i < Z + 3:
            own(i - 3)
        if 4 <= i < Z + 4:
            own_column(i - 4, in_src, in_at, in_recv)
            relay_column(i - 4, in_at, relay_ins, x_in_recv, in_recv)
            near(i - 4)
        if 5 <= i:
            far(i - 5)

    wait_recv(rows, row_recv)
    total = rows[0]
    for step in range(1, DP):
        total = total + rows[step]
    dense[...] = total
    load_counts.wait()

    for n, k in enumerate((0, 1, 2, 3, 4, 5, 7, 6)):
        slots = slots_from(k)
        wait_recv(outs.at[sibling, slots], core_recv.at[k, 0])
        wait_recv(outs.at[2 * ahead + 1 - c, slots], core_recv.at[k, 1])
        wait_recv(outs.at[2 * behind + 1 - c, slots], core_recv.at[k, 2])
        wait_recv(outs.at[2 * across + 1 - c, slots], core_recv.at[k, 3])
        wait_recv(ins.at[slots], in_recv.at[k])
        from_z = lax.rem(z + Z - wave(k), Z)
        live = []
        for dx in range(X):
            block = ins[slot_of(from_z, dx)]
            slot = BF16_ROWS * lax.broadcasted_iota(jnp.int32, block.shape, 0) + lax.broadcasted_iota(jnp.int32, block.shape, 1)
            count = counts[lax.rem(x + X - dx, X) * Z + from_z, e]
            live.append(jnp.where(slot < count, block, jnp.zeros_like(block)))
        left = jnp.stack(live, axis=1)
        right = outs[:, slots]
        product = lax.dot_general(
            left.reshape(-1, left.shape[-1]),
            right.reshape(-1, right.shape[-1]),
            (((0,), (0,)), ((), ())),
            preferred_element_type=jnp.float32,
        )
        if n == 0:
            grad[...] = product
        else:
            grad[...] += product

    def wait_send(ref, sem):
        remote(ref, ref, sem, sem, d, e).wait_send()

    wait_send(outs.at[0, pl.ds(0, Z * (X - 1))], to_x)
    wait_send(ins.at[pl.ds(0, Z * (X - 1))], to_x)
    wait_send(outs.at[0, pl.ds(0, (Z - 1) * X)], to_z)
    wait_send(ins.at[pl.ds(0, (Z - 1) * X)], to_z)
    wait_send(rows.at[pl.ds(0, DP - 1)], to_rows)
    wait_send(outs.at[pl.ds(0, 3)], to_y)
    wait_send(outs.at[pl.ds(0, 4)], to_core)


def per_device(
    dense_partials,
    dense_param,
    dense_m,
    dense_v,
    sent_inputs,
    sent_outputs,
    counts,
    expert_param,
    expert_m,
    expert_v,
):
    blocks, slots, width_in = sent_inputs.shape
    width_out = sent_outputs.shape[2]
    part = slots // DP
    dense_rows, dense_width = dense_partials.shape[1] // DP, dense_partials.shape[2]
    dma = pltpu.SemaphoreType.DMA
    expert_grad, dense_grad = pl.pallas_call(
        exchange,
        name="exchange",
        out_shape=(
            jax.ShapeDtypeStruct((width_in, width_out), jnp.float32),
            jax.ShapeDtypeStruct((dense_rows, dense_width), jnp.float32),
        ),
        in_specs=[pl.BlockSpec(memory_space=pltpu.HBM)] * 4,
        out_specs=(pl.BlockSpec(memory_space=pltpu.VMEM),) * 2,
        scratch_shapes=[
            pltpu.SMEM(counts.shape, counts.dtype),
            pltpu.VMEM((blocks, DP, part, width_in), jnp.bfloat16),
            pltpu.VMEM((DP, blocks, part, width_out), jnp.bfloat16),
            pltpu.VMEM((Z - 1, X - 1, DP, part, width_in), jnp.bfloat16),
            pltpu.VMEM((Z - 1, X - 1, part, width_out), jnp.bfloat16),
            pltpu.VMEM((DP, dense_rows, dense_width), jnp.float32),
            dma,
            dma((5,)),
            dma((Z - 1,)),
            dma((Z - 1,)),
            dma((Z,)),
            dma((Z,)),
            dma,
            dma((Z, 3)),
            dma((Z, 4)),
        ],
        cost_estimate=pl.CostEstimate(
            flops=2 * blocks * slots * width_in * width_out,
            bytes_accessed=2 * blocks * slots * (width_in + width_out),
            transcendentals=0,
        ),
        compiler_params=pltpu.CompilerParams(collective_id=0, has_side_effects=True, vmem_limit_bytes=48 << 20),
    )(
        counts,
        dense_partials.reshape(DP, dense_rows, dense_width),
        sent_inputs.reshape(blocks, DP, part, width_in),
        sent_outputs.reshape(blocks, DP, part, width_out),
    )
    dp_new, dm_new, dv_new = adamw(dense_param, dense_m, dense_v, dense_grad)
    ep_new, em_new, ev_new = adamw(expert_param, expert_m, expert_v, expert_grad[None])
    return (dp_new, dm_new, dv_new, ep_new, em_new, ev_new)


def solution(mesh):
    in_specs = (
        P("dp", None, "expert"),
        P("dp", "expert"),
        P("dp", "expert"),
        P("dp", "expert"),
        P("expert", None, "dp"),
        P("expert", None, None),
        P(),
        P("expert", "dp", None),
        P("expert", "dp", None),
        P("expert", "dp", None),
    )
    out_specs = (
        P("dp", "expert"),
        P("dp", "expert"),
        P("dp", "expert"),
        P("expert", "dp", None),
        P("expert", "dp", None),
        P("expert", "dp", None),
    )
    return jax.shard_map(per_device, mesh=mesh, in_specs=in_specs, out_specs=out_specs, check_vma=False)
```

time: 100 us -> 97.2 us (0.972)
  Pallas kernels: 92.3 us -> 89.5 us
    pallas_call x1, Pallas kernels: 92.3 us -> 89.5 us  [per_device(): pl.pallas_call(exchange, name='exchange', out_shape=(jax.ShapeDtypeStruct...]
where the time goes in v3:
time: 97.2 us; the launch traced here: 97 us
  Pallas kernels  89.5 us (92%)
  other arithmetic  3.43 us (4%)
  local copies, waits for them, and re-layouts  3.37 us (3%)
    pallas_call x1, Pallas kernels, per_device(): pl.pallas_call(exchange, name='exchange', out_shape=(jax.ShapeDtypeStruct...  89.5 us
    sub x2, other arithmetic, adamw(): param_new = param - 0.01 * (corrected / scaled + 0.1 * param)  3.43 us
    unnamed x18, local copies, waits for them, and re-layouts  3.37 us

profile of v3, /device:TPU:1, one launch (start us, length us, event | category | flops | bytes accessed | tf_op | source)
XLA Modules:
  0.0 97.0 jit_solution(6556821168763357928)
XLA Ops:
  0.6 0.0 copy-start
  0.6 1.6 %copy-done = bf16[32,128,256]{2,1,0:T(8,128)(2,1)S(1)} copy-done((bf16[32,128,256]{2,1,0:T(8,128)(2,1)S(1)}, bf16[32,128,256]{2,1,0:T(8,128)(2,1)}, u32[]{:S(2)}) %copy-start) | copy-done | bytes 2097176
  2.2 0.0 copy-start.1
  2.2 1.0 %copy-done.1 = f32[1,1024,128]{2,1,0:T(8,128)S(1)} copy-done((f32[1,1024,128]{2,1,0:T(8,128)S(1)}, f32[1,1024,128]{2,1,0:T(8,128)}, u32[]{:S(2)}) %copy-start.1) | copy-done | bytes 524312
  3.3 0.0 copy-start.2
  3.3 0.7 copy-done.2
  4.0 0.0 copy-start.3
  4.0 0.0 copy-start.4
  4.0 0.0 copy-start.5
  4.0 89.5 %exchange.1 = (f32[256,1408]{1,0:T(8,128)S(1)}, f32[128,128]{1,0:T(8,128)S(1)}) custom-call(s32[32,32]{1,0:T(8,128)S(1)} %copy-done.2, f32[8,128,128]{2,1,0:T(8,128)S(1)} %bitcast.12, bf16[32,8,16,256]{3,2,1,0:T(8,128)(2,1)S(1)} %bitcast.11, bf16[32,8,16,1408]{3,2,1,0:T(8,128)(2,1)} %bitcast.13), custom_call_target="tpu_custom_call" | custom-call | flops 2952790016 | bytes 13631488 | tf_op jit(solution)/shard_map/exchange/pallas_call | solution.py:231
  93.5 0.0 copy-done.3
  93.5 0.0 copy-done.4
  93.5 0.0 copy-done.5
  93.5 0.0 copy-start.6
  93.6 0.0 copy-start.7
  93.6 0.0 copy-start.8
  93.6 2.7 %multiply_subtract_fusion = (f32[1,256,1408]{2,1,0:T(8,128)}, f32[1,256,1408]{2,1,0:T(8,128)}, f32[1,256,1408]{2,1,0:T(8,128)}) fusion(f32[1,256,1408]{2,1,0:T(8,128)S(1)} %copy-done.3, f32[256,1408]{1,0:T(8,128)S(1)} %get-tuple-element.9, f32[1,256,1408]{2,1,0:T(8,128)S(1)} %copy-done.4, f32[1,256,1408]{2,1,0:T(8,128)S(1)} %copy-done.5), kind=kLoop, calls=%fused_computation.4 | loop fusion | flops 5406720 | bytes 10092544 | tf_op jit(solution)/shard_map/sub | solution.py:19
  96.3 0.0 copy-done.6
  96.3 0.0 copy-done.7
  96.3 0.0 copy-done.8
  96.3 0.7 multiply_subtract_fusion.1
Async XLA Ops:
  0.6 1.6 %copy-start = (bf16[32,128,256]{2,1,0:T(8,128)(2,1)S(1)}, bf16[32,128,256]{2,1,0:T(8,128)(2,1)}, u32[]{:S(2)}) copy-start(bf16[32,128,256]{2,1,0:T(8,128)(2,1)} %param.14) | copy-start | bytes 6291460
  2.2 1.0 %copy-start.1 = (f32[1,1024,128]{2,1,0:T(8,128)S(1)}, f32[1,1024,128]{2,1,0:T(8,128)}, u32[]{:S(2)}) copy-start(f32[1,1024,128]{2,1,0:T(8,128)} %param.10) | copy-start | bytes 1572868
  3.3 0.7 copy-start.2
  4.0 89.5 %copy-start.3 = (f32[1,256,1408]{2,1,0:T(8,128)S(1)}, f32[1,256,1408]{2,1,0:T(8,128)}, u32[]{:S(2)}) copy-start(f32[1,256,1408]{2,1,0:T(8,128)} %param.17) | copy-start | bytes 4325380
  4.0 89.5 %copy-start.4 = (f32[1,256,1408]{2,1,0:T(8,128)S(1)}, f32[1,256,1408]{2,1,0:T(8,128)}, u32[]{:S(2)}) copy-start(f32[1,256,1408]{2,1,0:T(8,128)} %param.18) | copy-start | bytes 4325380
  4.0 89.5 %copy-start.5 = (f32[1,256,1408]{2,1,0:T(8,128)S(1)}, f32[1,256,1408]{2,1,0:T(8,128)}, u32[]{:S(2)}) copy-start(f32[1,256,1408]{2,1,0:T(8,128)} %param.19) | copy-start | bytes 4325380
  93.5 2.8 %copy-start.6 = (f32[128,128]{1,0:T(8,128)S(1)}, f32[128,128]{1,0:T(8,128)}, u32[]{:S(2)}) copy-start(f32[128,128]{1,0:T(8,128)} %param.11) | copy-start | bytes 196612
  93.6 2.8 %copy-start.7 = (f32[128,128]{1,0:T(8,128)S(1)}, f32[128,128]{1,0:T(8,128)}, u32[]{:S(2)}) copy-start(f32[128,128]{1,0:T(8,128)} %param.12) | copy-start | bytes 196612
  93.6 2.8 %copy-start.8 = (f32[128,128]{1,0:T(8,128)S(1)}, f32[128,128]{1,0:T(8,128)}, u32[]{:S(2)}) copy-start(f32[128,128]{1,0:T(8,128)} %param.13) | copy-start | bytes 196612

commit v4 on v3

--- a/solution.py
+++ b/solution.py
@@ -9,6 +9,7 @@
 X, Z, Y = 4, 8, 4
 DP = 2 * Y
 BF16_ROWS = 16
+STRETCHES = 8
 
 
 def adamw(param, moment, second, grad):
@@ -18,6 +19,25 @@
     scaled = jnp.sqrt(second_new / (1.0 - 0.95**10)) + 1e-08
     param_new = param - 0.01 * (corrected / scaled + 0.1 * param)
     return (param_new, moment_new, second_new)
+
+
+def update(dense_in, expert_in, dense_out, expert_out, dense_new, expert_new, sem):
+    copies = []
+
+    def rows_of(ins, news, outs, first, count):
+        span = pl.ds(first, count)
+        for new, out, value in zip(news, outs, adamw(*(ref[span] for ref in ins)), strict=True):
+            new[span] = value
+            copies.append(pltpu.make_async_copy(new.at[span], out.at[span], sem.at[len(copies)]))
+            copies[-1].start()
+
+    rows = expert_in[0].shape[0]
+    step = rows // STRETCHES
+    for i in range(STRETCHES):
+        rows_of(expert_in, expert_new, expert_out, i * step, step)
+    rows_of(dense_in, dense_new, dense_out, 0, dense_in[0].shape[0])
+    for copy in copies:
+        copy.wait()
 
 
 def wave(k):
@@ -261,14 +281,32 @@
         ),
         compiler_params=pltpu.CompilerParams(collective_id=0, has_side_effects=True, vmem_limit_bytes=48 << 20),
     )(
-        counts,
-        dense_partials.reshape(DP, dense_rows, dense_width),
-        sent_inputs.reshape(blocks, DP, part, width_in),
-        sent_outputs.reshape(blocks, DP, part, width_out),
+        *(
+            pltpu.with_memory_space_constraint(operand, pltpu.HBM)
+            for operand in (
+                counts,
+                dense_partials.reshape(DP, dense_rows, dense_width),
+                sent_inputs.reshape(blocks, DP, part, width_in),
+                sent_outputs.reshape(blocks, DP, part, width_out),
+            )
+        )
     )
-    dp_new, dm_new, dv_new = adamw(dense_param, dense_m, dense_v, dense_grad)
-    ep_new, em_new, ev_new = adamw(expert_param, expert_m, expert_v, expert_grad[None])
-    return (dp_new, dm_new, dv_new, ep_new, em_new, ev_new)
+    dense_state = (dense_param, dense_m, dense_v)
+    expert_state = tuple(leaf[0] for leaf in (expert_param, expert_m, expert_v))
+    dense_new, expert_new = pl.pallas_call(
+        update,
+        name="update",
+        out_shape=tuple(tuple(jax.ShapeDtypeStruct(leaf.shape, leaf.dtype) for leaf in state) for state in (dense_state, expert_state)),
+        in_specs=((pl.BlockSpec(memory_space=pltpu.VMEM),) * 4,) * 2,
+        out_specs=((pl.BlockSpec(memory_space=pl.ANY),) * 3,) * 2,
+        scratch_shapes=[
+            tuple(pltpu.VMEM(leaf.shape, leaf.dtype) for leaf in dense_state),
+            tuple(pltpu.VMEM(leaf.shape, leaf.dtype) for leaf in expert_state),
+            dma((3 * (STRETCHES + 1),)),
+        ],
+        compiler_params=pltpu.CompilerParams(vmem_limit_bytes=24 << 20),
+    )((*dense_state, dense_grad), (*expert_state, expert_grad))
+    return (*dense_new, *(leaf[None] for leaf in expert_new))
 
 
 def solution(mesh):

time: 97.2 us -> 93 us (0.957)
  other arithmetic: 3.43 us -> 0 us
  local copies, waits for them, and re-layouts: 3.37 us -> 0.03 us
  Pallas kernels: 89.5 us -> 92.2 us
    sub x2 -> x0, other arithmetic: 3.43 us -> none  [adamw(): param_new = param - 0.01 * (corrected / scaled + 0.1 * param)]
    unnamed x18 -> x12, local copies, waits for them, and re-layouts: 3.37 us -> 0.03 us
    pallas_call x0 -> x1, Pallas kernels: none -> 2.48 us  [per_device(): pl.pallas_call(update, name='update', out_shape=tuple((tuple((jax.ShapeDt...]
where the time goes in v4:
time: 93 us; the launch traced here: 92.9 us
  Pallas kernels  92.2 us (99%)
    pallas_call x1, Pallas kernels, per_device(): pl.pallas_call(exchange, name='exchange', out_shape=(jax.ShapeDtypeStruct...  89.7 us
    pallas_call x1, Pallas kernels, per_device(): pl.pallas_call(update, name='update', out_shape=tuple((tuple((jax.ShapeDt...  2.48 us

profile of v4, /device:TPU:1, one launch (start us, length us, event | category | flops | bytes accessed | tf_op | source)
XLA Modules:
  0.0 92.9 jit_solution(8823606956549717829)
XLA Ops:
  0.6 0.0 copy-start
  0.6 0.0 copy-start.1
  0.7 0.0 copy-start.2
  0.7 0.0 copy-start.3
  0.7 0.0 copy-start.4
  0.7 0.0 copy-start.5
  0.7 89.7 %exchange.1 = (f32[256,1408]{1,0:T(8,128)S(1)}, f32[128,128]{1,0:T(8,128)S(1)}) custom-call(s32[32,32]{1,0:T(8,128)} %counts_hbm.1, f32[8,128,128]{2,1,0:T(8,128)} %bitcast.14, bf16[32,8,16,256]{3,2,1,0:T(8,128)(2,1)} %bitcast.13, bf16[32,8,16,1408]{3,2,1,0:T(8,128)(2,1)} %bitcast.12), custom_call_target="tpu_custom_call" | custom-call | flops 2952790016 | bytes 13631488 | tf_op jit(solution)/shard_map/exchange/pallas_call | solution.py:251
  90.4 0.0 copy-done
  90.4 0.0 copy-done.1
  90.4 0.0 copy-done.2
  90.4 0.0 copy-done.3
  90.4 0.0 copy-done.4
  90.5 0.0 copy-done.5
  90.5 2.5 %update.1 = (f32[128,128]{1,0:T(8,128)}, f32[128,128]{1,0:T(8,128)}, f32[128,128]{1,0:T(8,128)}, f32[256,1408]{1,0:T(8,128)}, f32[256,1408]{1,0:T(8,128)}, /*index=5*/f32[256,1408]{1,0:T(8,128)}) custom-call(f32[128,128]{1,0:T(8,128)S(1)} %copy-done.3, f32[128,128]{1,0:T(8,128)S(1)} %copy-done.4, f32[128,128]{1,0:T(8,128)S(1)} %copy-done.5, ...), custom_call_target="tpu_custom_call" | custom-call | tf_op jit(solution)/shard_map/update/pallas_call | solution.py:296
Async XLA Ops:
  0.6 89.8 %copy-start = (f32[1,256,1408]{2,1,0:T(8,128)S(1)}, f32[1,256,1408]{2,1,0:T(8,128)}, u32[]{:S(2)}) copy-start(f32[1,256,1408]{2,1,0:T(8,128)} %param.17) | copy-start | bytes 4325380
  0.6 89.8 %copy-start.1 = (f32[1,256,1408]{2,1,0:T(8,128)S(1)}, f32[1,256,1408]{2,1,0:T(8,128)}, u32[]{:S(2)}) copy-start(f32[1,256,1408]{2,1,0:T(8,128)} %param.18) | copy-start | bytes 4325380
  0.7 89.8 %copy-start.2 = (f32[1,256,1408]{2,1,0:T(8,128)S(1)}, f32[1,256,1408]{2,1,0:T(8,128)}, u32[]{:S(2)}) copy-start(f32[1,256,1408]{2,1,0:T(8,128)} %param.19) | copy-start | bytes 4325380
  0.7 89.8 %copy-start.3 = (f32[128,128]{1,0:T(8,128)S(1)}, f32[128,128]{1,0:T(8,128)}, u32[]{:S(2)}) copy-start(f32[128,128]{1,0:T(8,128)} %dense_in_0_.1) | copy-start | bytes 196612
  0.7 89.8 %copy-start.4 = (f32[128,128]{1,0:T(8,128)S(1)}, f32[128,128]{1,0:T(8,128)}, u32[]{:S(2)}) copy-start(f32[128,128]{1,0:T(8,128)} %dense_in_1_.1) | copy-start | bytes 196612
  0.7 89.8 %copy-start.5 = (f32[128,128]{1,0:T(8,128)S(1)}, f32[128,128]{1,0:T(8,128)}, u32[]{:S(2)}) copy-start(f32[128,128]{1,0:T(8,128)} %dense_in_2_.1) | copy-start | bytes 196612

commit v5 on v4

--- a/solution.py
+++ b/solution.py
@@ -14,10 +14,9 @@
 
 def adamw(param, moment, second, grad):
     moment_new = 0.9 * moment + 0.1 * grad
-    second_new = 0.95 * second + 0.05 * grad * grad
-    corrected = moment_new / (1.0 - 0.9**10)
-    scaled = jnp.sqrt(second_new / (1.0 - 0.95**10)) + 1e-08
-    param_new = param - 0.01 * (corrected / scaled + 0.1 * param)
+    second_new = 0.95 * second + (0.05 * grad) * grad
+    scaled = jnp.sqrt(second_new * (1.0 / (1.0 - 0.95**10))) + 1e-08
+    param_new = (1.0 - 0.01 * 0.1) * param - (0.01 / (1.0 - 0.9**10)) * moment_new / scaled
     return (param_new, moment_new, second_new)
 
 
@@ -43,6 +42,9 @@
 def wave(k):
     half = (k + 1) // 2
     return 4 + half if k % 2 == 0 else 4 - half
+
+
+TAIL = (5, 6)
 
 
 def exchange(
@@ -58,13 +60,17 @@
     relay_ins,
     relay_outs,
     rows,
+    rows_core,
+    rows_hop,
     counts_sem,
     send,
     x_out_recv,
     x_in_recv,
     out_recv,
     in_recv,
+    tail_recv,
     row_recv,
+    hop_recv,
     y_recv,
     core_recv,
 ):
@@ -97,9 +103,9 @@
         pl.semaphore_signal(barrier, inc=1, device_id=(d, peer(0, dz)), device_id_type=MESH)
     for dx in range(1, X):
         pl.semaphore_signal(barrier, inc=1, device_id=(d, peer(dx, 0)), device_id_type=MESH)
-    for step in range(1, DP):
-        pl.semaphore_signal(barrier, inc=1, device_id=(lax.rem(d + step, DP), e), device_id_type=MESH)
-    pl.semaphore_wait(barrier, Z - 1 + X - 1 + DP - 1)
+    for there in (2 * ahead + c, 2 * behind + c, sibling):
+        pl.semaphore_signal(barrier, inc=1, device_id=(there, e), device_id_type=MESH)
+    pl.semaphore_wait(barrier, Z - 1 + X - 1 + 3)
 
     def slot_of(source_z, dx):
         return source_z * X + dx
@@ -146,10 +152,21 @@
     for k in range(Z):
         own_column(k, out_src, out_at, out_recv)
         to_columns(k, out_src, out_at, relay_outs, x_out_recv, out_recv)
-    for step in range(1, DP):
-        there = lax.rem(d + step, DP)
-        remote(partials.at[there], rows.at[d], to_rows, row_recv, there, e).start()
-    pltpu.make_async_copy(partials.at[d], rows.at[d], row_recv).start()
+    remote(partials.at[:, 1 - c], rows_core, to_rows, row_recv.at[0], sibling, e).start()
+    own_rows = pltpu.make_async_copy(partials.at[:, c], rows, row_recv.at[1])
+    own_rows.start()
+
+    def rows_of_chip():
+        own_rows.wait()
+        wait_recv(rows_core, row_recv.at[0])
+        rows[...] += rows_core[...]
+        remote(rows.at[across], rows_hop.at[0], to_rows, hop_recv.at[0], 2 * ahead + c, e).start()
+        remote(rows.at[behind], rows_hop.at[1], to_rows, hop_recv.at[1], 2 * behind + c, e).start()
+
+    def rows_of_two_chips():
+        wait_recv(rows_hop.at[0], hop_recv.at[0])
+        rows[ahead] += rows_hop[0]
+        remote(rows.at[ahead], rows_hop.at[2], to_rows, hop_recv.at[2], 2 * ahead + c, e).start()
 
     def own(k):
         piece = outs.at[d, slots_from(k)]
@@ -172,6 +189,14 @@
         wait_recv(piece, y_recv.at[k, 2])
         remote(piece, piece, to_core, core_recv.at[k, 3], sibling, e).start()
 
+    def send_tail(k):
+        there = peer(0, wave(k))
+        recv = tail_recv.at[k - TAIL[0]]
+        remote(in_src(there), ins.at[slot_of(z, 0)], to_z, recv.at[0], d, there).start()
+        wait_recv(relay_ins.at[k], x_in_recv.at[k])
+        for dx in range(1, X):
+            remote(relay_ins.at[k, dx - 1], ins.at[slot_of(z, dx)], to_z, recv.at[dx], d, there).start()
+
     for i in range(Z + 5):
         if i < Z:
             relay_column(i, out_at, relay_outs, x_out_recv, out_recv)
@@ -179,45 +204,61 @@
         if 3 <= i < Z + 3:
             own(i - 3)
         if 4 <= i < Z + 4:
-            own_column(i - 4, in_src, in_at, in_recv)
-            relay_column(i - 4, in_at, relay_ins, x_in_recv, in_recv)
+            if i - 4 in TAIL:
+                send_tail(i - 4)
+            else:
+                own_column(i - 4, in_src, in_at, in_recv)
+                relay_column(i - 4, in_at, relay_ins, x_in_recv, in_recv)
             near(i - 4)
         if 5 <= i:
             far(i - 5)
-
-    wait_recv(rows, row_recv)
-    total = rows[0]
-    for step in range(1, DP):
-        total = total + rows[step]
-    dense[...] = total
+        if i == 2:
+            rows_of_chip()
+        if i == 4:
+            rows_of_two_chips()
+
+    wait_recv(rows_hop.at[1], hop_recv.at[1])
+    wait_recv(rows_hop.at[2], hop_recv.at[2])
+    dense[...] = (rows[y] + rows_hop[1]) + rows_hop[2]
     load_counts.wait()
 
-    for n, k in enumerate((0, 1, 2, 3, 4, 5, 7, 6)):
+    def gathered(k):
         slots = slots_from(k)
         wait_recv(outs.at[sibling, slots], core_recv.at[k, 0])
         wait_recv(outs.at[2 * ahead + 1 - c, slots], core_recv.at[k, 1])
         wait_recv(outs.at[2 * behind + 1 - c, slots], core_recv.at[k, 2])
         wait_recv(outs.at[2 * across + 1 - c, slots], core_recv.at[k, 3])
-        wait_recv(ins.at[slots], in_recv.at[k])
-        from_z = lax.rem(z + Z - wave(k), Z)
-        live = []
-        for dx in range(X):
+
+    def product(pieces):
+        left, right = [], []
+        for k, dx in pieces:
+            from_z = lax.rem(z + Z - wave(k), Z)
             block = ins[slot_of(from_z, dx)]
             slot = BF16_ROWS * lax.broadcasted_iota(jnp.int32, block.shape, 0) + lax.broadcasted_iota(jnp.int32, block.shape, 1)
             count = counts[lax.rem(x + X - dx, X) * Z + from_z, e]
-            live.append(jnp.where(slot < count, block, jnp.zeros_like(block)))
-        left = jnp.stack(live, axis=1)
-        right = outs[:, slots]
-        product = lax.dot_general(
-            left.reshape(-1, left.shape[-1]),
-            right.reshape(-1, right.shape[-1]),
+            left.append(jnp.where(slot < count, block, jnp.zeros_like(block)).reshape(-1, block.shape[-1]))
+            right.append(outs[:, slot_of(from_z, dx)].reshape(-1, outs.shape[-1]))
+        return lax.dot_general(
+            jnp.concatenate(left, axis=0),
+            jnp.concatenate(right, axis=0),
             (((0,), (0,)), ((), ())),
             preferred_element_type=jnp.float32,
         )
-        if n == 0:
-            grad[...] = product
+
+    for k in (0, 1, 2, 3, 4, 7):
+        gathered(k)
+        wait_recv(ins.at[slots_from(k)], in_recv.at[k])
+        if k == 0:
+            grad[...] = product([(k, dx) for dx in range(X)])
         else:
-            grad[...] += product
+            grad[...] += product([(k, dx) for dx in range(X)])
+    for k in TAIL:
+        gathered(k)
+    for dx in range(X):
+        for k in TAIL:
+            piece = slot_of(lax.rem(z + Z - wave(k), Z), dx)
+            wait_recv(ins.at[piece], tail_recv.at[k - TAIL[0], dx])
+        grad[...] += product([(k, dx) for k in TAIL])
 
     def wait_send(ref, sem):
         remote(ref, ref, sem, sem, d, e).wait_send()
@@ -226,7 +267,8 @@
     wait_send(ins.at[pl.ds(0, Z * (X - 1))], to_x)
     wait_send(outs.at[0, pl.ds(0, (Z - 1) * X)], to_z)
     wait_send(ins.at[pl.ds(0, (Z - 1) * X)], to_z)
-    wait_send(rows.at[pl.ds(0, DP - 1)], to_rows)
+    wait_send(rows, to_rows)
+    wait_send(rows_hop, to_rows)
     wait_send(outs.at[pl.ds(0, 3)], to_y)
     wait_send(outs.at[pl.ds(0, 4)], to_core)
 
@@ -263,14 +305,18 @@
             pltpu.VMEM((DP, blocks, part, width_out), jnp.bfloat16),
             pltpu.VMEM((Z - 1, X - 1, DP, part, width_in), jnp.bfloat16),
             pltpu.VMEM((Z - 1, X - 1, part, width_out), jnp.bfloat16),
-            pltpu.VMEM((DP, dense_rows, dense_width), jnp.float32),
+            pltpu.VMEM((Y, dense_rows, dense_width), jnp.float32),
+            pltpu.VMEM((Y, dense_rows, dense_width), jnp.float32),
+            pltpu.VMEM((3, dense_rows, dense_width), jnp.float32),
             dma,
             dma((5,)),
             dma((Z - 1,)),
             dma((Z - 1,)),
             dma((Z,)),
             dma((Z,)),
-            dma,
+            dma((len(TAIL), X)),
+            dma((2,)),
+            dma((3,)),
             dma((Z, 3)),
             dma((Z, 4)),
         ],
@@ -285,7 +331,7 @@
             pltpu.with_memory_space_constraint(operand, pltpu.HBM)
             for operand in (
                 counts,
-                dense_partials.reshape(DP, dense_rows, dense_width),
+                dense_partials.reshape(Y, 2, dense_rows, dense_width),
                 sent_inputs.reshape(blocks, DP, part, width_in),
                 sent_outputs.reshape(blocks, DP, part, width_out),
             )

time: 93 us -> 90.8 us (0.976)
  Pallas kernels: 92.2 us -> 90 us
    pallas_call x1, Pallas kernels: 89.7 us -> 87.5 us  [per_device(): pl.pallas_call(exchange, name='exchange', out_shape=(jax.ShapeDtypeStruct...]
where the time goes in v5:
time: 90.8 us; the launch traced here: 90.7 us
  Pallas kernels  90 us (99%)
    pallas_call x1, Pallas kernels, per_device(): pl.pallas_call(exchange, name='exchange', out_shape=(jax.ShapeDtypeStruct...  87.5 us
    pallas_call x1, Pallas kernels, per_device(): pl.pallas_call(update, name='update', out_shape=tuple((tuple((jax.ShapeDt...  2.47 us

profile of v5, /device:TPU:1, one launch (start us, length us, event | category | flops | bytes accessed | tf_op | source)
XLA Modules:
  0.0 90.7 jit_solution(703659431692426468)
XLA Ops:
  0.6 0.0 copy-start
  0.6 0.0 copy-start.1
  0.7 0.0 copy-start.2
  0.7 0.0 copy-start.3
  0.7 0.0 copy-start.4
  0.7 0.0 copy-start.5
  0.7 87.5 %exchange.1 = (f32[256,1408]{1,0:T(8,128)S(1)}, f32[128,128]{1,0:T(8,128)S(1)}) custom-call(s32[32,32]{1,0:T(8,128)} %counts_hbm.1, f32[4,2,128,128]{3,2,1,0:T(8,128)} %bitcast.14, bf16[32,8,16,256]{3,2,1,0:T(8,128)(2,1)} %bitcast.13, bf16[32,8,16,1408]{3,2,1,0:T(8,128)(2,1)} %bitcast.12), custom_call_target="tpu_custom_call" | custom-call | flops 2952790016 | bytes 13631488 | tf_op jit(solution)/shard_map/exchange/pallas_call | solution.py:293
  88.2 0.0 copy-done
  88.2 0.0 copy-done.1
  88.2 0.0 copy-done.2
  88.3 0.0 copy-done.3
  88.3 0.0 copy-done.4
  88.3 0.0 copy-done.5
  88.3 2.5 %update.1 = (f32[128,128]{1,0:T(8,128)}, f32[128,128]{1,0:T(8,128)}, f32[128,128]{1,0:T(8,128)}, f32[256,1408]{1,0:T(8,128)}, f32[256,1408]{1,0:T(8,128)}, /*index=5*/f32[256,1408]{1,0:T(8,128)}) custom-call(f32[128,128]{1,0:T(8,128)S(1)} %copy-done.3, f32[128,128]{1,0:T(8,128)S(1)} %copy-done.4, f32[128,128]{1,0:T(8,128)S(1)} %copy-done.5, ...), custom_call_target="tpu_custom_call" | custom-call | tf_op jit(solution)/shard_map/update/pallas_call | solution.py:342
Async XLA Ops:
  0.6 87.6 %copy-start = (f32[1,256,1408]{2,1,0:T(8,128)S(1)}, f32[1,256,1408]{2,1,0:T(8,128)}, u32[]{:S(2)}) copy-start(f32[1,256,1408]{2,1,0:T(8,128)} %param.17) | copy-start | bytes 4325380
  0.6 87.6 %copy-start.1 = (f32[1,256,1408]{2,1,0:T(8,128)S(1)}, f32[1,256,1408]{2,1,0:T(8,128)}, u32[]{:S(2)}) copy-start(f32[1,256,1408]{2,1,0:T(8,128)} %param.18) | copy-start | bytes 4325380
  0.7 87.6 %copy-start.2 = (f32[1,256,1408]{2,1,0:T(8,128)S(1)}, f32[1,256,1408]{2,1,0:T(8,128)}, u32[]{:S(2)}) copy-start(f32[1,256,1408]{2,1,0:T(8,128)} %param.19) | copy-start | bytes 4325380
  0.7 87.6 %copy-start.3 = (f32[128,128]{1,0:T(8,128)S(1)}, f32[128,128]{1,0:T(8,128)}, u32[]{:S(2)}) copy-start(f32[128,128]{1,0:T(8,128)} %dense_in_0_.1) | copy-start | bytes 196612
  0.7 87.6 %copy-start.4 = (f32[128,128]{1,0:T(8,128)S(1)}, f32[128,128]{1,0:T(8,128)}, u32[]{:S(2)}) copy-start(f32[128,128]{1,0:T(8,128)} %dense_in_1_.1) | copy-start | bytes 196612
  0.7 87.6 %copy-start.5 = (f32[128,128]{1,0:T(8,128)S(1)}, f32[128,128]{1,0:T(8,128)}, u32[]{:S(2)}) copy-start(f32[128,128]{1,0:T(8,128)} %dense_in_2_.1) | copy-start | bytes 196612

commit v6 on v5

--- a/solution.py
+++ b/solution.py
@@ -9,7 +9,7 @@
 X, Z, Y = 4, 8, 4
 DP = 2 * Y
 BF16_ROWS = 16
-STRETCHES = 8
+STRETCHES = (2, 4, 6, 8, 12)
 
 
 def adamw(param, moment, second, grad):
@@ -30,11 +30,11 @@
             copies.append(pltpu.make_async_copy(new.at[span], out.at[span], sem.at[len(copies)]))
             copies[-1].start()
 
-    rows = expert_in[0].shape[0]
-    step = rows // STRETCHES
-    for i in range(STRETCHES):
-        rows_of(expert_in, expert_new, expert_out, i * step, step)
     rows_of(dense_in, dense_new, dense_out, 0, dense_in[0].shape[0])
+    first = 0
+    for groups in STRETCHES:
+        rows_of(expert_in, expert_new, expert_out, first, 8 * groups)
+        first += 8 * groups
     for copy in copies:
         copy.wait()
 
@@ -96,15 +96,20 @@
     def peer(dx, dz):
         return lax.rem(x + dx, X) * Z + lax.rem(z + dz, Z)
 
-    load_counts = pltpu.make_async_copy(counts_hbm, counts, counts_sem)
-    load_counts.start()
     barrier = pltpu.get_barrier_semaphore()
-    for dz in range(1, Z):
+    for dz in (4, 3, 5, 2, 6, 1, 7):
         pl.semaphore_signal(barrier, inc=1, device_id=(d, peer(0, dz)), device_id_type=MESH)
-    for dx in range(1, X):
+    for dx in (2, 1, 3):
         pl.semaphore_signal(barrier, inc=1, device_id=(d, peer(dx, 0)), device_id_type=MESH)
     for there in (2 * ahead + c, 2 * behind + c, sibling):
         pl.semaphore_signal(barrier, inc=1, device_id=(there, e), device_id_type=MESH)
+    slot = z * X
+    load_counts = pltpu.make_async_copy(counts_hbm, counts, counts_sem)
+    own_rows = pltpu.make_async_copy(partials.at[:, c], rows, row_recv.at[1])
+    own_outs = pltpu.make_async_copy(outputs.at[e, d], outs.at[d, slot], out_recv.at[Z - 1])
+    own_ins = pltpu.make_async_copy(inputs.at[e], ins.at[slot], in_recv.at[Z - 1])
+    for copy in (load_counts, own_rows, own_outs, own_ins):
+        copy.start()
     pl.semaphore_wait(barrier, Z - 1 + X - 1 + 3)
 
     def slot_of(source_z, dx):
@@ -129,8 +134,6 @@
         mine = buffer(pl.ds(slot_of(z, 0), 1)).at[0]
         if wave(k):
             remote(src_of(there), mine, to_z, recv.at[k], d, there).start()
-        else:
-            pltpu.make_async_copy(src_of(there), mine, recv.at[k]).start()
 
     def relay_column(k, buffer, relay, x_recv, recv):
         if wave(k):
@@ -153,8 +156,6 @@
         own_column(k, out_src, out_at, out_recv)
         to_columns(k, out_src, out_at, relay_outs, x_out_recv, out_recv)
     remote(partials.at[:, 1 - c], rows_core, to_rows, row_recv.at[0], sibling, e).start()
-    own_rows = pltpu.make_async_copy(partials.at[:, c], rows, row_recv.at[1])
-    own_rows.start()
 
     def rows_of_chip():
         own_rows.wait()
@@ -348,7 +349,7 @@
         scratch_shapes=[
             tuple(pltpu.VMEM(leaf.shape, leaf.dtype) for leaf in dense_state),
             tuple(pltpu.VMEM(leaf.shape, leaf.dtype) for leaf in expert_state),
-            dma((3 * (STRETCHES + 1),)),
+            dma((3 * (len(STRETCHES) + 1),)),
         ],
         compiler_params=pltpu.CompilerParams(vmem_limit_bytes=24 << 20),
     )((*dense_state, dense_grad), (*expert_state, expert_grad))

time: 90.8 us -> 90.7 us (level)
  no operation moved by 1% of the time
where the time goes in v6:
time: 90.7 us; the launch traced here: 90.6 us
  Pallas kernels  89.9 us (99%)
    pallas_call x1, Pallas kernels, per_device(): pl.pallas_call(exchange, name='exchange', out_shape=(jax.ShapeDtypeStruct...  87.5 us
    pallas_call x1, Pallas kernels, per_device(): pl.pallas_call(update, name='update', out_shape=tuple((tuple((jax.ShapeDt...  2.37 us

profile of v6, /device:TPU:1, one launch (start us, length us, event | category | flops | bytes accessed | tf_op | source)
XLA Modules:
  0.0 90.6 jit_solution(3853129234386017140)
XLA Ops:
  0.6 0.0 copy-start
  0.6 0.0 copy-start.1
  0.7 0.0 copy-start.2
  0.7 0.0 copy-start.3
  0.7 0.0 copy-start.4
  0.7 0.0 copy-start.5
  0.7 87.5 %exchange.1 = (f32[256,1408]{1,0:T(8,128)S(1)}, f32[128,128]{1,0:T(8,128)S(1)}) custom-call(s32[32,32]{1,0:T(8,128)} %counts_hbm.1, f32[4,2,128,128]{3,2,1,0:T(8,128)} %bitcast.14, bf16[32,8,16,256]{3,2,1,0:T(8,128)(2,1)} %bitcast.13, bf16[32,8,16,1408]{3,2,1,0:T(8,128)(2,1)} %bitcast.12), custom_call_target="tpu_custom_call" | custom-call | flops 2952790016 | bytes 13631488 | tf_op jit(solution)/shard_map/exchange/pallas_call | solution.py:294
  88.2 0.0 copy-done
  88.2 0.0 copy-done.1
  88.2 0.0 copy-done.2
  88.2 0.0 copy-done.3
  88.3 0.0 copy-done.4
  88.3 0.0 copy-done.5
  88.3 2.4 %update.1 = (f32[128,128]{1,0:T(8,128)}, f32[128,128]{1,0:T(8,128)}, f32[128,128]{1,0:T(8,128)}, f32[256,1408]{1,0:T(8,128)}, f32[256,1408]{1,0:T(8,128)}, /*index=5*/f32[256,1408]{1,0:T(8,128)}) custom-call(f32[128,128]{1,0:T(8,128)S(1)} %copy-done.3, f32[128,128]{1,0:T(8,128)S(1)} %copy-done.4, f32[128,128]{1,0:T(8,128)S(1)} %copy-done.5, ...), custom_call_target="tpu_custom_call" | custom-call | tf_op jit(solution)/shard_map/update/pallas_call | solution.py:343
Async XLA Ops:
  0.6 87.6 %copy-start = (f32[1,256,1408]{2,1,0:T(8,128)S(1)}, f32[1,256,1408]{2,1,0:T(8,128)}, u32[]{:S(2)}) copy-start(f32[1,256,1408]{2,1,0:T(8,128)} %param.17) | copy-start | bytes 4325380
  0.6 87.6 %copy-start.1 = (f32[1,256,1408]{2,1,0:T(8,128)S(1)}, f32[1,256,1408]{2,1,0:T(8,128)}, u32[]{:S(2)}) copy-start(f32[1,256,1408]{2,1,0:T(8,128)} %param.18) | copy-start | bytes 4325380
  0.7 87.6 %copy-start.2 = (f32[1,256,1408]{2,1,0:T(8,128)S(1)}, f32[1,256,1408]{2,1,0:T(8,128)}, u32[]{:S(2)}) copy-start(f32[1,256,1408]{2,1,0:T(8,128)} %param.19) | copy-start | bytes 4325380
  0.7 87.6 %copy-start.3 = (f32[128,128]{1,0:T(8,128)S(1)}, f32[128,128]{1,0:T(8,128)}, u32[]{:S(2)}) copy-start(f32[128,128]{1,0:T(8,128)} %dense_in_0_.1) | copy-start | bytes 196612
  0.7 87.6 %copy-start.4 = (f32[128,128]{1,0:T(8,128)S(1)}, f32[128,128]{1,0:T(8,128)}, u32[]{:S(2)}) copy-start(f32[128,128]{1,0:T(8,128)} %dense_in_1_.1) | copy-start | bytes 196612
  0.7 87.6 %copy-start.5 = (f32[128,128]{1,0:T(8,128)S(1)}, f32[128,128]{1,0:T(8,128)}, u32[]{:S(2)}) copy-start(f32[128,128]{1,0:T(8,128)} %dense_in_2_.1) | copy-start | bytes 196612

commit v7 on v6

--- a/solution.py
+++ b/solution.py
@@ -198,31 +198,6 @@
         for dx in range(1, X):
             remote(relay_ins.at[k, dx - 1], ins.at[slot_of(z, dx)], to_z, recv.at[dx], d, there).start()
 
-    for i in range(Z + 5):
-        if i < Z:
-            relay_column(i, out_at, relay_outs, x_out_recv, out_recv)
-            to_columns(i, in_src, in_at, relay_ins, x_in_recv, in_recv)
-        if 3 <= i < Z + 3:
-            own(i - 3)
-        if 4 <= i < Z + 4:
-            if i - 4 in TAIL:
-                send_tail(i - 4)
-            else:
-                own_column(i - 4, in_src, in_at, in_recv)
-                relay_column(i - 4, in_at, relay_ins, x_in_recv, in_recv)
-            near(i - 4)
-        if 5 <= i:
-            far(i - 5)
-        if i == 2:
-            rows_of_chip()
-        if i == 4:
-            rows_of_two_chips()
-
-    wait_recv(rows_hop.at[1], hop_recv.at[1])
-    wait_recv(rows_hop.at[2], hop_recv.at[2])
-    dense[...] = (rows[y] + rows_hop[1]) + rows_hop[2]
-    load_counts.wait()
-
     def gathered(k):
         slots = slots_from(k)
         wait_recv(outs.at[sibling, slots], core_recv.at[k, 0])
@@ -246,13 +221,44 @@
             preferred_element_type=jnp.float32,
         )
 
-    for k in (0, 1, 2, 3, 4, 7):
+    def multiply(k):
         gathered(k)
         wait_recv(ins.at[slots_from(k)], in_recv.at[k])
+        whole = product([(k, dx) for dx in range(X)])
         if k == 0:
-            grad[...] = product([(k, dx) for dx in range(X)])
+            grad[...] = whole
         else:
-            grad[...] += product([(k, dx) for dx in range(X)])
+            grad[...] += whole
+
+    for i in range(Z + 5):
+        if i < Z:
+            relay_column(i, out_at, relay_outs, x_out_recv, out_recv)
+            to_columns(i, in_src, in_at, relay_ins, x_in_recv, in_recv)
+        if 3 <= i < Z + 3:
+            own(i - 3)
+        if 4 <= i < Z + 4:
+            if i - 4 in TAIL:
+                send_tail(i - 4)
+            else:
+                own_column(i - 4, in_src, in_at, in_recv)
+                relay_column(i - 4, in_at, relay_ins, x_in_recv, in_recv)
+            near(i - 4)
+        for k in {11: (0, 1), 12: (2, 3)}.get(i, ()):
+            multiply(k)
+        if 5 <= i:
+            far(i - 5)
+        if i == 2:
+            load_counts.wait()
+            rows_of_chip()
+        if i == 4:
+            rows_of_two_chips()
+
+    wait_recv(rows_hop.at[1], hop_recv.at[1])
+    wait_recv(rows_hop.at[2], hop_recv.at[2])
+    dense[...] = (rows[y] + rows_hop[1]) + rows_hop[2]
+
+    for k in (4, 7):
+        multiply(k)
     for k in TAIL:
         gathered(k)
     for dx in range(X):

time: 90.7 us -> 90.7 us (level)
  no operation moved by 1% of the time
where the time goes in v7:
time: 90.7 us; the launch traced here: 90.6 us
  Pallas kernels  89.9 us (99%)
    pallas_call x1, Pallas kernels, per_device(): pl.pallas_call(exchange, name='exchange', out_shape=(jax.ShapeDtypeStruct...  87.5 us
    pallas_call x1, Pallas kernels, per_device(): pl.pallas_call(update, name='update', out_shape=tuple((tuple((jax.ShapeDt...  2.37 us

profile of v7, /device:TPU:1, one launch (start us, length us, event | category | flops | bytes accessed | tf_op | source)
XLA Modules:
  0.0 90.6 jit_solution(3127647010877170519)
XLA Ops:
  0.6 0.0 copy-start
  0.6 0.0 copy-start.1
  0.7 0.0 copy-start.2
  0.7 0.0 copy-start.3
  0.7 0.0 copy-start.4
  0.7 0.0 copy-start.5
  0.7 87.5 %exchange.1 = (f32[256,1408]{1,0:T(8,128)S(1)}, f32[128,128]{1,0:T(8,128)S(1)}) custom-call(s32[32,32]{1,0:T(8,128)} %counts_hbm.1, f32[4,2,128,128]{3,2,1,0:T(8,128)} %bitcast.14, bf16[32,8,16,256]{3,2,1,0:T(8,128)(2,1)} %bitcast.13, bf16[32,8,16,1408]{3,2,1,0:T(8,128)(2,1)} %bitcast.12), custom_call_target="tpu_custom_call" | custom-call | flops 2952790016 | bytes 13631488 | tf_op jit(solution)/shard_map/exchange/pallas_call | solution.py:300
  88.2 0.0 copy-done
  88.2 0.0 copy-done.1
  88.2 0.0 copy-done.2
  88.2 0.0 copy-done.3
  88.3 0.0 copy-done.4
  88.3 0.0 copy-done.5
  88.3 2.4 %update.1 = (f32[128,128]{1,0:T(8,128)}, f32[128,128]{1,0:T(8,128)}, f32[128,128]{1,0:T(8,128)}, f32[256,1408]{1,0:T(8,128)}, f32[256,1408]{1,0:T(8,128)}, /*index=5*/f32[256,1408]{1,0:T(8,128)}) custom-call(f32[128,128]{1,0:T(8,128)S(1)} %copy-done.3, f32[128,128]{1,0:T(8,128)S(1)} %copy-done.4, f32[128,128]{1,0:T(8,128)S(1)} %copy-done.5, ...), custom_call_target="tpu_custom_call" | custom-call | tf_op jit(solution)/shard_map/update/pallas_call | solution.py:349
Async XLA Ops:
  0.6 87.6 %copy-start = (f32[1,256,1408]{2,1,0:T(8,128)S(1)}, f32[1,256,1408]{2,1,0:T(8,128)}, u32[]{:S(2)}) copy-start(f32[1,256,1408]{2,1,0:T(8,128)} %param.17) | copy-start | bytes 4325380
  0.6 87.6 %copy-start.1 = (f32[1,256,1408]{2,1,0:T(8,128)S(1)}, f32[1,256,1408]{2,1,0:T(8,128)}, u32[]{:S(2)}) copy-start(f32[1,256,1408]{2,1,0:T(8,128)} %param.18) | copy-start | bytes 4325380
  0.7 87.6 %copy-start.2 = (f32[1,256,1408]{2,1,0:T(8,128)S(1)}, f32[1,256,1408]{2,1,0:T(8,128)}, u32[]{:S(2)}) copy-start(f32[1,256,1408]{2,1,0:T(8,128)} %param.19) | copy-start | bytes 4325380
  0.7 87.6 %copy-start.3 = (f32[128,128]{1,0:T(8,128)S(1)}, f32[128,128]{1,0:T(8,128)}, u32[]{:S(2)}) copy-start(f32[128,128]{1,0:T(8,128)} %dense_in_0_.1) | copy-start | bytes 196612
  0.7 87.6 %copy-start.4 = (f32[128,128]{1,0:T(8,128)S(1)}, f32[128,128]{1,0:T(8,128)}, u32[]{:S(2)}) copy-start(f32[128,128]{1,0:T(8,128)} %dense_in_1_.1) | copy-start | bytes 196612
  0.7 87.6 %copy-start.5 = (f32[128,128]{1,0:T(8,128)S(1)}, f32[128,128]{1,0:T(8,128)}, u32[]{:S(2)}) copy-start(f32[128,128]{1,0:T(8,128)} %dense_in_2_.1) | copy-start | bytes 196612
